TPU v7x, 32 devices: a whole 2x2x4 slice. The times are simulated.
32 devices in a mesh: dp: 8 (over y, x, core), tensor: 4 (over z).
Axes of the slice: x: 2, y: 2, z: 4, core: 2. Of those that a mesh axis runs over, the one named last changes fastest.
Arguments:
- tokens: bfloat16 [32, 2048, 768], P('dp', 'tensor'), may hold values from -6 to 6
- segment_ids: int32 [32, 2048], P('dp'), may hold values from 0 to 4, as said below
- selected: int32 [32, 256], P('dp'), may hold values from 0 to 2047, as said below
- w_router: bfloat16 [768], replicated, may hold values from -0.21875 to 0.21875
- gain_one: float32 [768], replicated, may hold values from 0.5 to 1.5
- w_query: bfloat16 [768, 768], P(None, 'tensor'), may hold values from -0.21875 to 0.21875
- w_key: bfloat16 [768, 768], P(None, 'tensor'), may hold values from -0.21875 to 0.21875
- w_value: bfloat16 [768, 768], P(None, 'tensor'), may hold values from -0.21875 to 0.21875
- w_out: bfloat16 [768, 768], P('tensor'), may hold values from -0.75 to 0.75
- gain_two: float32 [768], replicated, may hold values from 0.5 to 1.5
- w_up: bfloat16 [768, 3072], P(None, 'tensor'), may hold values from -0.21875 to 0.21875
- w_down: bfloat16 [3072, 768], P('tensor'), may hold values from -0.109375 to 0.109375
- grad_out: bfloat16 [32, 2048, 768], P('dp', 'tensor'), may hold values from -6 to 6
Outputs:
- layer_out: bfloat16 [32, 2048, 768], P('dp', 'tensor')
- grad_tokens: bfloat16 [32, 2048, 768], P('dp', 'tensor')
- grad_router: float32 [768], replicated
- grad_gain_one: float32 [768], replicated
- grad_query: float32 [768, 768], P(None, 'tensor')
- grad_key: float32 [768, 768], P(None, 'tensor')
- grad_value: float32 [768, 768], P(None, 'tensor')
- grad_out_proj: float32 [768, 768], P('tensor')
- grad_gain_two: float32 [768], replicated
- grad_up: float32 [768, 3072], P(None, 'tensor')
- grad_down: float32 [3072, 768], P('tensor')
Inputs may be any that keep to these rules, and one draw needn't show every extreme that they name: `selected`: in each row the 256 positions are distinct and increasing, and every row names position 0 and position 2047. `segment_ids`: document numbers never fall along a row; each row starts with document 0 and ends with document 4.
All inputs are finite; a program needn't handle non-finite values.
Results may differ from a plain program's by a relative error of at most 0.018.
Values may be sent and summed in bfloat16 or wider, within the bound.
No kernel may reach another device: no remote copies, remote signals or barrier semaphores. Data moves between devices by JAX's collectives and lax.ppermute only.
A program may use at most 128 MiB of HBM per device.

v0:
```python
import jax
import jax.numpy as jnp
from jax import lax
from jax.sharding import PartitionSpec as P

HD = 64


EPS = 1e-06
NEG = -1e30


def rms_norm(values, gain):
    return values * lax.rsqrt(jnp.mean(values * values, -1, keepdims=True) + EPS) * gain


def block_scores(query_blk, key_blk, tag_blk):
    score_scale = query_blk.shape[-1] ** (-0.5)
    raw_scores = (
        jnp.einsum("qhd,khd->hqk", query_blk, key_blk, preferred_element_type=jnp.float32)
        * score_scale
    )
    position = jnp.arange(tag_blk.shape[0])
    allowed = (tag_blk[:, None] == tag_blk[None, :]) & (position[:, None] >= position[None, :])
    return jnp.where(allowed[None], raw_scores, NEG)


def attend_block(block_in):
    query_blk, key_blk, value_blk, tag_blk = block_in
    scores = block_scores(query_blk, key_blk, tag_blk)
    row_top = jnp.max(scores, -1)
    shifted = jnp.exp(scores - row_top[..., None])
    row_total = jnp.sum(shifted, -1)
    prob_table = shifted / row_total[..., None]
    mixed = jnp.einsum(
        "hqk,khd->qhd",
        prob_table.astype(jnp.bfloat16),
        value_blk,
        preferred_element_type=jnp.float32,
    )
    return (mixed.astype(jnp.bfloat16), row_top + jnp.log(row_total))


def attend_back(block_in):
    query_blk, key_blk, value_blk, tag_blk, lse_blk, grad_blk = block_in
    score_scale = query_blk.shape[-1] ** (-0.5)
    scores = block_scores(query_blk, key_blk, tag_blk)
    prob_table = jnp.exp(scores - lse_blk[..., None])
    d_probs = jnp.einsum("qhd,khd->hqk", grad_blk, value_blk, preferred_element_type=jnp.float32)
    d_value = jnp.einsum(
        "hqk,qhd->khd",
        prob_table.astype(jnp.bfloat16),
        grad_blk,
        preferred_element_type=jnp.float32,
    )
    d_scores = prob_table * (d_probs - jnp.sum(d_probs * prob_table, -1, keepdims=True))
    d_scores = d_scores.astype(jnp.bfloat16)
    d_query = (
        jnp.einsum("hqk,khd->qhd", d_scores, key_blk, preferred_element_type=jnp.float32)
        * score_scale
    )
    d_key = (
        jnp.einsum("hqk,qhd->khd", d_scores, query_blk, preferred_element_type=jnp.float32)
        * score_scale
    )
    return (d_query, d_key, d_value)


def local(
    tokens,
    segment_ids,
    selected,
    w_router,
    gain_one,
    w_query,
    w_key,
    w_value,
    w_out,
    gain_two,
    w_up,
    w_down,
    grad_out,
):
    row_count, local_len, model_width = tokens.shape
    pick_count = selected.shape[1]
    full_len = segment_ids.shape[1]
    flat_count = row_count * pick_count
    local_start = lax.axis_index("tensor") * local_len
    local_pos = local_start + jnp.arange(local_len, dtype=jnp.int32)
    hit_local = selected[:, :, None] == local_pos[None, None, :]
    hit_bf = hit_local.astype(jnp.bfloat16)
    whole_tokens, whole_grads = (
        lax.all_gather(tokens, "tensor", axis=1, tiled=True),
        lax.all_gather(grad_out, "tensor", axis=1, tiled=True),
    )
    full_pos = jnp.arange(full_len, dtype=jnp.int32)
    hit_whole = (selected[:, :, None] == full_pos[None, None, :]).astype(jnp.bfloat16)
    chosen = jnp.einsum("rkl,rld->rkd", hit_whole, whole_tokens, preferred_element_type=jnp.float32)
    chosen_grad = jnp.einsum(
        "rkl,rld->rkd", hit_whole, whole_grads, preferred_element_type=jnp.float32
    )
    sel_tokens = chosen.reshape(flat_count, model_width)
    sel_bf = sel_tokens.astype(jnp.bfloat16)
    sel_grads = chosen_grad.reshape(flat_count, model_width)
    gate_score = jnp.dot(sel_bf, w_router, preferred_element_type=jnp.float32)
    picked_seg = jnp.take_along_axis(segment_ids, selected, axis=1)
    row_tags = (picked_seg + 8 * jnp.arange(row_count, dtype=jnp.int32)[:, None]).reshape(
        flat_count
    )
    head_count = w_query.shape[1] // HD
    group_rows = min(row_count, max(1, 512 // pick_count))
    block_count = row_count // group_rows
    block_len = group_rows * pick_count

    def to_blocks(values):
        return values.reshape(block_count, block_len, head_count, HD)

    tag_blocks = row_tags.reshape(block_count, block_len)
    normed = rms_norm(sel_tokens, gain_one)
    normed_bf = normed.astype(jnp.bfloat16)
    query_bf = jnp.dot(normed_bf, w_query, preferred_element_type=jnp.float32).astype(jnp.bfloat16)
    key_bf = jnp.dot(normed_bf, w_key, preferred_element_type=jnp.float32).astype(jnp.bfloat16)
    value_bf = jnp.dot(normed_bf, w_value, preferred_element_type=jnp.float32).astype(jnp.bfloat16)
    query_blocks = to_blocks(query_bf)
    key_blocks = to_blocks(key_bf)
    value_blocks = to_blocks(value_bf)
    mixed_blocks, lse_blocks = lax.map(
        attend_block, (query_blocks, key_blocks, value_blocks, tag_blocks)
    )
    mixed_bf = mixed_blocks.reshape(flat_count, head_count * HD)
    attn_part = jnp.dot(mixed_bf, w_out, preferred_element_type=jnp.float32)
    attended = lax.psum(attn_part.astype(jnp.bfloat16), "tensor").astype(jnp.float32)
    middle = sel_tokens + attended
    normed_two = rms_norm(middle, gain_two)
    normed_two_bf = normed_two.astype(jnp.bfloat16)
    hidden_pre = jnp.dot(normed_two_bf, w_up, preferred_element_type=jnp.float32)
    hidden_bf = jax.nn.gelu(hidden_pre).astype(jnp.bfloat16)
    branch_part = jnp.dot(hidden_bf, w_down, preferred_element_type=jnp.float32)
    branch = lax.psum(branch_part.astype(jnp.bfloat16), "tensor").astype(jnp.float32)
    delta_sum = attended + branch
    updated = sel_tokens + gate_score[:, None] * delta_sum
    covered = jnp.sum(hit_local.astype(jnp.int32), axis=1)[:, :, None] > 0

    def place(values, initial):
        values_bf = values.astype(jnp.bfloat16).reshape(row_count, pick_count, model_width)
        placed = jnp.einsum("rkl,rkd->rld", hit_bf, values_bf, preferred_element_type=jnp.float32)
        return jnp.where(covered, placed.astype(jnp.bfloat16), initial)

    layer_out = place(updated, tokens)
    d_gate = jnp.sum(sel_grads * delta_sum, -1)
    d_branch = (gate_score[:, None] * sel_grads).astype(jnp.bfloat16)
    grad_down = jnp.dot(hidden_bf.T, d_branch, preferred_element_type=jnp.float32)
    d_hidden = jnp.dot(d_branch, w_down.T, preferred_element_type=jnp.float32)
    unused, gelu_back = jax.vjp(jax.nn.gelu, hidden_pre)
    d_pre = gelu_back(d_hidden)[0].astype(jnp.bfloat16)
    grad_up = jnp.dot(normed_two_bf.T, d_pre, preferred_element_type=jnp.float32)
    d_normed_two = lax.psum(
        jnp.dot(d_pre, w_up.T, preferred_element_type=jnp.float32).astype(jnp.bfloat16), "tensor"
    ).astype(jnp.float32)
    unused, norm_two_back = jax.vjp(rms_norm, middle, gain_two)
    d_middle, grad_gain_two = norm_two_back(d_normed_two)
    d_attended_bf = (d_middle + gate_score[:, None] * sel_grads).astype(jnp.bfloat16)
    grad_out_proj = jnp.dot(mixed_bf.T, d_attended_bf, preferred_element_type=jnp.float32)
    d_mixed = jnp.dot(d_attended_bf, w_out.T, preferred_element_type=jnp.float32).astype(
        jnp.bfloat16
    )
    d_query, d_key, d_value = lax.map(
        attend_back,
        (query_blocks, key_blocks, value_blocks, tag_blocks, lse_blocks, to_blocks(d_mixed)),
    )
    d_query_bf = d_query.reshape(flat_count, head_count * HD).astype(jnp.bfloat16)
    d_key_bf = d_key.reshape(flat_count, head_count * HD).astype(jnp.bfloat16)
    d_value_bf = d_value.reshape(flat_count, head_count * HD).astype(jnp.bfloat16)
    grad_query = jnp.dot(normed_bf.T, d_query_bf, preferred_element_type=jnp.float32)
    grad_key = jnp.dot(normed_bf.T, d_key_bf, preferred_element_type=jnp.float32)
    grad_value = jnp.dot(normed_bf.T, d_value_bf, preferred_element_type=jnp.float32)
    d_normed_part = (
        jnp.dot(d_query_bf, w_query.T, preferred_element_type=jnp.float32)
        + jnp.dot(d_key_bf, w_key.T, preferred_element_type=jnp.float32)
        + jnp.dot(d_value_bf, w_value.T, preferred_element_type=jnp.float32)
    )
    d_normed = lax.psum(d_normed_part.astype(jnp.bfloat16), "tensor").astype(jnp.float32)
    unused, norm_one_back = jax.vjp(rms_norm, sel_tokens, gain_one)
    d_first, grad_gain_one = norm_one_back(d_normed)
    d_selected = (
        sel_grads + d_middle + d_first + d_gate[:, None] * w_router.astype(jnp.float32)[None, :]
    )
    grad_router = jnp.dot(d_gate, sel_tokens, precision=lax.Precision.HIGHEST)
    grad_tokens = place(d_selected, grad_out)
    (
        grad_router,
        grad_gain_one,
        grad_query,
        grad_key,
        grad_value,
        grad_out_proj,
        grad_gain_two,
        grad_up,
        grad_down,
    ) = lax.psum(
        (
            grad_router,
            grad_gain_one,
            grad_query,
            grad_key,
            grad_value,
            grad_out_proj,
            grad_gain_two,
            grad_up,
            grad_down,
        ),
        "dp",
    )
    return (
        layer_out,
        grad_tokens,
        grad_router,
        grad_gain_one,
        grad_query,
        grad_key,
        grad_value,
        grad_out_proj,
        grad_gain_two,
        grad_up,
        grad_down,
    )


def solution(mesh):
    placed = (
        P("dp", "tensor", None),
        P("dp", None),
        P("dp", None),
        P(),
        P(),
        P(None, "tensor"),
        P(None, "tensor"),
        P(None, "tensor"),
        P("tensor", None),
        P(),
        P(None, "tensor"),
        P("tensor", None),
        P("dp", "tensor", None),
    )
    return jax.shard_map(
        local,
        mesh=mesh,
        in_specs=placed,
        out_specs=(
            P("dp", "tensor", None),
            P("dp", "tensor", None),
            P(),
            P(),
            P(None, "tensor"),
            P(None, "tensor"),
            P(None, "tensor"),
            P("tensor", None),
            P(),
            P(None, "tensor"),
            P("tensor", None),
        ),
        check_vma=False,
    )
```

profile of v0, /device:TPU:0, one launch (start us, length us, event | category | flops | bytes accessed | tf_op | source)
XLA Modules:
  0.0 887.7 jit_solution(17930622858457963630)
XLA Ops:
  9.5 9.1 %gather_fusion = s32[1024]{0:T(1024)S(1)} fusion(s32[4,2048]{1,0:T(4,128)S(1)} %copy-done.2, s32[1024]{0:T(1024)S(1)} %bitcast.228), kind=kCustom, calls=%fused_computation | custom fusion | bytes 16384 | tf_op jit(solution)/shard_map/jit(take_along_axis)/gather | solution.py:106
  18.7 211.9 %all-gather.3.cloned.1.call-done = bf16[4,2048,768]{2,1,0:T(8,128)(2,1)} async-done(((bf16[4,512,768]{2,1,0:T(8,128)(2,1)}), bf16[4,2048,768]{2,1,0:T(8,128)(2,1)}) %all-gather.3.cloned.1.call-update) | async-done | bytes 12582928 | tf_op jit(solution)/shard_map/all_gather | solution.py:93
  230.6 6.7 multiply_reduce_fusion.2
  237.9 1.0 copy-done.3
  240.3 2.5 convolution_convert_fusion.6
  242.8 1.3 reshape.279
  244.2 2.4 convolution_convert_fusion.5
  246.9 6.8 while.26
  247.1 0.8 fusion.165
  247.9 0.7 fusion.166
  248.6 1.1 fusion.167
  250.5 0.8 fusion.165
  252.0 1.1 fusion.167
  253.7 0.7 copy-done.27
  254.5 1.6 copy.42
  256.1 2.9 convolution_convert_fusion.2
  259.0 2.4 fusion.84
  261.6 187.0 %all-gather.5.cloned.1.call-done = bf16[4,2048,768]{2,1,0:T(8,128)(2,1)} async-done(((bf16[4,512,768]{2,1,0:T(8,128)(2,1)}), bf16[4,2048,768]{2,1,0:T(8,128)(2,1)}) %all-gather.5.cloned.1.call-update) | async-done | bytes 12582928 | tf_op jit(solution)/shard_map/all_gather | solution.py:94
  448.6 6.5 fusion.51
  455.2 1.6 copy-done.6
  457.3 3.1 fusion.95
  460.4 58.5 %all-reduce.8.cloned.1.call-done = bf16[1024,768]{1,0:T(8,128)(2,1)} async-done(((bf16[1024,768]{1,0:T(8,128)(2,1)}), bf16[1024,768]{1,0:T(8,128)(2,1)}) %all-reduce.8.cloned.1.call-update) | async-done | bytes 1572880 | tf_op jit(solution)/shard_map/psum | solution.py:132
  518.9 3.0 multiply_reduce_fusion.1
  523.1 1.4 copy-done.63
  524.5 2.9 fusion.73
  527.5 2.7 convolution_convert_fusion
  530.1 3.2 convolution_convert_fusion.1
  534.0 3.4 multiply_convert_fusion.1
  537.4 116.6 %all-reduce.14.cloned.1.call-done = (bf16[1024,768]{1,0:T(8,128)(2,1)}, bf16[1024,768]{1,0:T(8,128)(2,1)}) async-done(((bf16[1024,768]{1,0:T(8,128)(2,1)}, bf16[1024,768]{1,0:T(8,128)(2,1)}), (bf16[1024,768]{1,0:T(8,128)(2,1)}, bf16[1024,768]{1,0:T(8,128)(2,1)})) %all-reduce.14.cloned.1.call-update) | async-done | bytes 3145744 | tf_op jit(solution)/shard_map/psum | solution.py:139
  654.0 6.5 fusion.65
  660.6 1.8 add_convert_fusion.1
  662.4 1.1 copy-done.11
  664.2 1.0 reshape.286
  665.2 1.0 copy.45
  666.3 11.4 %while.27 = (s32[]{:T(128)}, bf16[2,512,3,64]{1,3,2,0:T(8,128)(2,1)}, bf16[2,512,3,64]{1,3,2,0:T(8,128)(2,1)}, bf16[2,512,3,64]{1,3,2,0:T(8,128)(2,1)}, bf16[2,5...) while((s32[]{:T(128)}, ...), condition=%wide.region_13.14_spmd, body=%wide.region_11.13_spmd.sunk | while | flops 511375872 | bytes 36154660 | solution.py:167
  666.6 1.0 subtract_exponential_fusion.3
  668.9 0.8 multiply_convert_fusion.8
  671.2 0.7 copy-done.34
  672.2 1.0 subtract_exponential_fusion.3
  674.6 0.8 multiply_convert_fusion.8
  676.9 0.7 copy-done.34
  677.7 1.5 copy.49
  679.2 1.4 copy.47
  682.4 1.8 add_convert_fusion
  684.6 5.7 fusion.94
  690.3 2.9 fusion.99
  693.2 1.3 fusion.98
  694.5 1.3 fusion.101
  695.8 1.3 fusion.100
  697.1 1.3 fusion.102
  699.5 3.7 convolution_reduce_fusion
  703.3 3.9 convert_select_fusion.1
  707.3 45.3 %all-reduce.10.cloned.1.call-done = bf16[1024,768]{1,0:T(8,128)(2,1)} async-done(((bf16[1024,768]{1,0:T(8,128)(2,1)}), bf16[1024,768]{1,0:T(8,128)(2,1)}) %all-reduce.10.cloned.1.call-update) | async-done | bytes 1572880 | tf_op jit(solution)/shard_map/psum | solution.py:182
  752.5 3.5 fusion.66
  756.0 23.8 %all-reduce = (f32[768]{0:T(1024)}, f32[768]{0:T(1024)}, f32[768]{0:T(1024)}) all-reduce(f32[768]{0:T(1024)S(1)} %convolution_reduce_fusion, f32[768]{0:T(1024)S(1)} %get-tuple-element.144, f32[768]{0:T(1024)S(1)} %copy-done.56), channel_id=1, replica_groups=mesh['dp'=8,'tensor'=4] {'dp'}, use_global_device_ids=true, to_apply=%region_17.18 | all-reduce | flops 2304 | bytes 18432 | tf_op jit(solution)/shard_map/psum | solution.py:200
  779.8 5.2 fusion.76
  785.0 2.5 convert_select_fusion
  787.5 83.3 %all-reduce.12.cloned.1.call-done = (f32[768,192]{0,1:T(8,128)}, f32[768,192]{0,1:T(8,128)}, f32[768,192]{0,1:T(8,128)}, f32[192,768]{1,0:T(8,128)}, f32[768,768]{1,0:T(8,128)}, /*index=5*/f32[768,768]{1,0:T(8,128)}) async-done(((f32[768,192]{0,1:T(8,128)}, f32[768,192]{0,1:T(8,128)}, f32[768,192]{0,1:T(8,128)}, f32[192,768]{1,0:T(8,128)}, f32[768,768]{1,0:T(8,128)}, /*index=5*/f32[768,768]{1,0:T(8,128)}), ...) | async-done | bytes 7077904 | tf_op jit(solution)/shard_map/psum | solution.py:200
  870.8 2.1 copy.99
  872.9 1.9 copy.100
  874.8 1.9 copy.101
  876.7 0.8 copy.102
  877.6 1.4 copy.103
  879.0 1.4 copy.104
  (214 shorter events, 19.9 us)
Async XLA Ops:
  7.2 516.0 %copy-start = (bf16[768,768]{1,0:T(8,128)(2,1)S(1)}, bf16[768,768]{1,0:T(8,128)(2,1)}, u32[]{:S(2)}) copy-start(bf16[768,768]{1,0:T(8,128)(2,1)} %param.27) | copy-start | bytes 3538948
  7.2 1.7 copy-start.59
  7.2 2.3 copy-start.50
  7.2 2.3 copy-start.2
  7.2 223.3 %all-gather.3.cloned.1.call-start = ((), (), s32[]{:S(2)}) async-start(), calls=%async_computation | async-start | bytes 15728640 | tf_op jit(solution)/shard_map/all_gather | solution.py:93
  8.0 440.6 %all-gather.5.cloned.1.call-start = ((), (), s32[]{:S(2)}) async-start(), calls=%async_computation.2 | async-start | bytes 15728640 | tf_op jit(solution)/shard_map/all_gather | solution.py:94
  8.7 510.2 %all-reduce.8.cloned.1.call-start = ((), (), s32[]{:S(2)}) async-start(), calls=%async_computation.1 | async-start | bytes 3145728 | tf_op jit(solution)/shard_map/psum | solution.py:132
  18.7 220.3 %copy-start.41 = (f32[768]{0:T(1024)S(1)}, f32[768]{0:T(1024)}, u32[]{:S(2)}) copy-start(f32[768]{0:T(1024)} %param.21) | copy-start | bytes 9220
  237.3 1.7 copy-start.3
  237.3 2.0 copy-start.38
  237.9 1.4 copy-start.52
  237.9 2.1 copy-start.43
  239.3 3.5 copy-start.24
  244.1 2.8 copy-start.26
  254.5 6.9 copy-start.13
  254.5 4.5 copy-start.58
  256.1 5.3 copy-start.15
  261.4 193.8 %copy-start.45 = (f32[1,1024]{1,0:T(1,128)}, f32[1,1024]{1,0:T(1,128)S(1)}, u32[]{:S(2)}) copy-start(f32[1,1024]{1,0:T(1,128)S(1)} %fusion.84) | copy-start | bytes 12292
  261.4 392.6 %all-reduce.14.cloned.1.call-start = ((), (), s32[]{:S(2)}) async-start(), calls=%async_computation.5 | async-start | bytes 6291456 | tf_op jit(solution)/shard_map/psum | solution.py:139
  455.1 1.6 copy-start.6
  455.1 2.2 copy-start.61
  457.3 3.1 copy-start.21
  460.4 62.1 %copy-start.42 = (f32[768]{0:T(1024)S(1)}, f32[768]{0:T(1024)}, u32[]{:S(2)}) copy-start(f32[768]{0:T(1024)} %param.26) | copy-start | bytes 9220
  518.9 3.6 copy-start.4
  518.9 3.8 copy-start.8
  522.6 1.9 copy-start.63
  524.5 2.9 copy-start.22
  527.4 2.7 copy-start.64
  527.4 2.7 copy-start.66
  527.5 2.7 copy-start.62
  533.3 120.7 %copy-start.46 = (f32[1,1024]{1,0:T(1,128)S(1)}, f32[1,1024]{1,0:T(1,128)}, u32[]{:S(2)}) copy-start(f32[1,1024]{1,0:T(1,128)} %copy-done.45) | copy-start | bytes 12292
  533.3 219.2 %all-reduce.10.cloned.1.call-start = ((), (), s32[]{:S(2)}) async-start(), calls=%async_computation.3 | async-start | bytes 3145728 | tf_op jit(solution)/shard_map/psum | solution.py:182
  654.0 6.5 copy-start.55
  654.0 6.5 copy-start.5
  654.0 6.5 copy-start.7
  654.0 6.6 copy-start.10
  660.6 1.8 copy-start.48
  660.6 2.9 copy-start.35
  663.5 2.7 copy-start.14
  663.5 2.8 copy-start.40
  666.3 1.2 copy-start.28
  668.9 1.6 copy-start.33
  672.0 1.2 copy-start.28
  674.6 1.6 copy-start.33
  677.6 3.0 copy-start.32
  677.7 3.5 copy-start.37
  680.6 1.2 copy-start.39
  681.1 1.3 copy-start.36
  684.2 186.6 %all-reduce.12.cloned.1.call-start = ((), (), s32[]{:S(2)}) async-start(), calls=%async_computation.4 | async-start | bytes 14155776 | tf_op jit(solution)/shard_map/psum | solution.py:200
  684.5 5.8 copy-start.23
  684.6 5.8 copy-start.65
  690.3 2.9 copy-start.12
  690.3 2.9 copy-start.16
  690.3 4.2 copy-start.9
  699.1 4.2 copy-start.17
  703.3 49.2 %copy-start.44 = (f32[1024]{0:T(1024)S(1)}, f32[1024]{0:T(1024)}, u32[]{:S(2)}) copy-start(f32[1024]{0:T(1024)} %copy-done.43) | copy-start | bytes 12292
  707.3 48.7 %copy-start.56 = (f32[768]{0:T(1024)S(1)}, f32[768]{0:T(1024)}, u32[]{:S(2)}) copy-start(f32[768]{0:T(1024)} %get-tuple-element.142) | copy-start | bytes 9220
  707.3 72.5 %copy-start.53 = (f32[1,2,4,128]{3,1,2,0:T(2,128)S(1)}, f32[1,2,4,128]{3,1,2,0:T(2,128)}, u32[]{:S(2)}) copy-start(f32[1,2,4,128]{3,1,2,0:T(2,128)} %copy-done.52) | copy-start | bytes 12292
  707.3 72.5 %copy-start.49 = (f32[1024]{0:T(1024)S(1)}, f32[1024]{0:T(1024)}, u32[]{:S(2)}) copy-start(f32[1024]{0:T(1024)} %copy-done.48) | copy-start | bytes 12292
  779.8 5.2 copy-start.18
  870.8 5.9 copy-start.25
  870.8 6.7 copy-start.20
  876.7 2.2 copy-start.19
  877.6 2.8 copy-start.1
  (15 other events, 12.2 us)
Sparse Core Ops, SparseCore 0:
  9.6 220.9 all-gather.2
  232.1 216.3 all-gather.4
  451.5 67.2 all-reduce.7
  533.4 120.4 all-reduce.13
  684.4 68.1 all-reduce.9
  757.6 113.1 all-reduce.11
where the time goes:
time: 895 us; the launch traced here: 888 us
  waiting for transfers between devices  704 us (79%)
  matrix products  73.5 us (8%)
  local copies, waits for them, and re-layouts  39.5 us (4%)
  other arithmetic  30.6 us (3%)
  blocking collectives  23.8 us (3%)
  between operations  15.3 us (2%)
    all_gather x1, waiting for transfers between devices, local(): lax.all_gather(tokens, 'tensor', axis=1, tiled=True)  212 us
    all_gather x1, waiting for transfers between devices, local(): lax.all_gather(grad_out, 'tensor', axis=1, tiled=True)  187 us
    psum x1, waiting for transfers between devices, local(): lax.psum(branch_part.astype(jnp.bfloat16), 'tensor').astype(jnp.float32)  117 us
    psum x1, waiting for transfers between devices, local(): lax.psum((grad_router, grad_gain_one, grad_query, grad_key, grad_value, g...  83.3 us
    psum x1, waiting for transfers between devices, local(): lax.psum(attn_part.astype(jnp.bfloat16), 'tensor').astype(jnp.float32)  58.5 us
    psum x1, waiting for transfers between devices, local(): lax.psum(d_normed_part.astype(jnp.bfloat16), 'tensor').astype(jnp.float32)  45.3 us
    psum x1, blocking collectives, local(): lax.psum((grad_router, grad_gain_one, grad_query, grad_key, grad_value, g...  23.8 us
    unnamed x137, local copies, waits for them, and re-layouts  18.7 us
  transfers between devices with their start and end apart: 6, of which 6 were waited for; matrix products, arithmetic and copies ran while one was open for 10% of the time, Pallas kernels for 0%

commit v1 on v0

v1 whole, which is shorter than its diff:
```python
import functools

import jax
import jax.numpy as jnp
from jax import lax
from jax.experimental import pallas as pl
from jax.experimental.pallas import tpu as pltpu
from jax.sharding import PartitionSpec as P


HD = 64
EPS = 1e-06
NEG = -1e30
EXTRA = 16
VMEM_LIMIT = 48 * 1024 * 1024
F32 = jnp.float32
BF16 = jnp.bfloat16


def nn(left, right):
    return lax.dot_general(left, right, (((1,), (0,)), ((), ())), preferred_element_type=F32)


def nt(left, right):
    return lax.dot_general(left, right, (((1,), (1,)), ((), ())), preferred_element_type=F32)


def tn(left, right):
    return lax.dot_general(left, right, (((0,), (0,)), ((), ())), preferred_element_type=F32)


def inv_rms(values):
    return lax.rsqrt(jnp.mean(values * values, -1, keepdims=True) + EPS)


def load_weights(core, own, other, table):
    pieces = len(own)
    tensor_size, types, heads, width, _ = own[0].shape
    for which, refs in ((core, own), (1 - core, other)):
        for c in range(pieces):
            for z in range(tensor_size):
                for t in range(types):
                    for h in range(heads):
                        start = (z * heads + h) * HD + c * width
                        table[2 * which + t, start : start + width, :] = refs[c][z, t, h]


def allowed_mask(tag_col, tag_row):
    count = tag_row.shape[1]
    query = lax.broadcasted_iota(jnp.int32, (count, count), 0)
    key = lax.broadcasted_iota(jnp.int32, (count, count), 1)
    return (tag_col == tag_row) & (query >= key)


def attend_kernel(pieces, core_ref, x_ref, tag_col, tag_row, gain_one, gain_two, router, *refs):
    own, other = refs[:pieces], refs[pieces : 2 * pieces]
    q_ref, k_ref, v_ref, mixed_ref, lse_ref, att_ref, normed_two_ref, gate_ref, table = refs[
        2 * pieces :
    ]
    load_weights(core_ref[0], own, other, table)
    x = x_ref[...].astype(F32)
    gate_ref[...] = jnp.sum(x * router[...], -1, keepdims=True)
    normed = (x * inv_rms(x) * gain_one[...]).astype(BF16)
    q_ref[...] = nt(normed, table[0]).astype(BF16)
    k_ref[...] = nt(normed, table[1]).astype(BF16)
    v_ref[...] = nt(normed, table[2]).astype(BF16)
    allowed = allowed_mask(tag_col[...], tag_row[...])
    heads = q_ref.shape[1] // HD
    for h in range(heads):
        part = slice(h * HD, (h + 1) * HD)
        scores = jnp.where(allowed, nt(q_ref[:, part], k_ref[:, part]) * HD**-0.5, NEG)
        top = jnp.max(scores, -1, keepdims=True)
        shifted = jnp.exp(scores - top)
        total = jnp.sum(shifted, -1, keepdims=True)
        probs = (shifted / total).astype(BF16)
        mixed_ref[:, part] = nn(probs, v_ref[:, part]).astype(BF16)
        lse_ref[:, h : h + 1] = top + jnp.log(total)
    attended = nn(mixed_ref[...], table[3])
    att_ref[...] = attended
    middle = x + attended
    normed_two_ref[...] = (middle * inv_rms(middle) * gain_two[...]).astype(BF16)


GELU_A = 0.7978845608028654
GELU_B = 0.044715


def hidden_kernel(pieces, first, last, n2_own, n2_oth, db_own, db_oth, *refs):
    weights = refs[:pieces]
    refs = refs[pieces:]
    if not first:
        dn_in, br_in = refs[:2]
        refs = refs[2:]
    grads = refs[:pieces]
    outs = refs[pieces:]
    count = n2_own.shape[0]
    n2 = jnp.concatenate([n2_own[...], n2_oth[...]], 0)
    db = jnp.concatenate([db_own[...], db_oth[...]], 0)
    d_normed, branch = None, None
    for i in range(pieces):
        tensor_size, _, width, model = weights[i].shape
        rows = tensor_size * width
        up = weights[i][:, 0].reshape(rows, model)
        down = weights[i][:, 1].reshape(rows, model)
        pre = nt(n2, up)
        inner = jnp.tanh(GELU_A * (pre + GELU_B * pre * pre * pre))
        hidden = (0.5 * pre * (1.0 + inner)).astype(BF16)
        slope = 0.5 * (1.0 + inner) + 0.5 * pre * (1.0 - inner * inner) * (
            GELU_A * (1.0 + 3.0 * GELU_B * pre * pre)
        )
        d_pre = (nt(db, down) * slope).astype(BF16)
        branch_part = nn(hidden, down)
        d_normed_part = nn(d_pre, up)
        branch = branch_part if branch is None else branch + branch_part
        d_normed = d_normed_part if d_normed is None else d_normed + d_normed_part
        grads[i][:, 0] = tn(d_pre, n2).astype(BF16).reshape(tensor_size, width, model)
        grads[i][:, 1] = tn(hidden, db).astype(BF16).reshape(tensor_size, width, model)
    if not first:
        d_normed = d_normed + dn_in[...]
        branch = branch + br_in[...]
    if last:
        dn_own, dn_send, br_own, br_send = outs
        dn_own[...] = d_normed[:count]
        dn_send[...] = d_normed[count:].astype(BF16)
        br_own[...] = branch[:count]
        br_send[...] = branch[count:].astype(BF16)
    else:
        dn_out, br_out = outs
        dn_out[...] = d_normed
        br_out[...] = branch


def back_kernel(
    pieces,
    core_ref,
    x_ref,
    cg_ref,
    gate_ref,
    att_ref,
    br_own,
    br_recv,
    dn_own,
    dn_recv,
    q_ref,
    k_ref,
    v_ref,
    mixed_ref,
    lse_ref,
    tag_col,
    tag_row,
    gain_one,
    gain_two,
    router,
    *refs,
):
    own, other = refs[:pieces], refs[pieces : 2 * pieces]
    keep_ref, send_ref, chosen_ref, table, grads, dq_ref, dk_ref, dv_ref = refs[2 * pieces :]
    core = core_ref[0]
    load_weights(core, own, other, table)
    tensor_size, types, per_shard, width, model = own[0].shape
    x = x_ref[...].astype(F32)
    chosen_grad = cg_ref[...].astype(F32)
    gate = gate_ref[...]
    attended = att_ref[...]
    middle = x + attended
    d_normed_two = dn_own[...] + dn_recv[...].astype(F32)
    scale_two = inv_rms(middle)
    grad_gain_two = jnp.sum(d_normed_two * middle * scale_two, 0, keepdims=True)
    weighted = d_normed_two * gain_two[...]
    d_middle = weighted * scale_two - middle * (
        scale_two * scale_two * scale_two * jnp.mean(weighted * middle, -1, keepdims=True)
    )
    d_attended = (d_middle + gate * chosen_grad).astype(BF16)
    grads[3] = tn(mixed_ref[...], d_attended).astype(BF16)
    d_mixed = nt(d_attended, table[3]).astype(BF16)
    allowed = allowed_mask(tag_col[...], tag_row[...])
    heads = q_ref.shape[1] // HD
    for h in range(heads):
        part = slice(h * HD, (h + 1) * HD)
        q, k, v = q_ref[:, part], k_ref[:, part], v_ref[:, part]
        dm = d_mixed[:, part]
        scores = jnp.where(allowed, nt(q, k) * HD**-0.5, NEG)
        probs = jnp.exp(scores - lse_ref[:, h : h + 1])
        d_probs = nt(dm, v)
        dv_ref[:, part] = tn(probs.astype(BF16), dm).astype(BF16)
        d_scores = probs * (d_probs - jnp.sum(d_probs * probs, -1, keepdims=True))
        d_scores = d_scores.astype(BF16)
        dq_ref[:, part] = (nn(d_scores, k) * HD**-0.5).astype(BF16)
        dk_ref[:, part] = (tn(d_scores, q) * HD**-0.5).astype(BF16)
    scale_one = inv_rms(x)
    normed = (x * scale_one * gain_one[...]).astype(BF16)
    grads[0] = tn(dq_ref[...], normed).astype(BF16)
    grads[1] = tn(dk_ref[...], normed).astype(BF16)
    grads[2] = tn(dv_ref[...], normed).astype(BF16)
    d_normed = nn(dq_ref[...], table[0]) + nn(dk_ref[...], table[1]) + nn(dv_ref[...], table[2])
    grad_gain_one = jnp.sum(d_normed * x * scale_one, 0, keepdims=True)
    weighted = d_normed * gain_one[...]
    d_first = weighted * scale_one - x * (
        scale_one * scale_one * scale_one * jnp.mean(weighted * x, -1, keepdims=True)
    )
    branch = br_own[...] + br_recv[...].astype(F32)
    d_gate = jnp.sum(chosen_grad * (attended + branch), -1, keepdims=True)
    chosen_ref[...] = (chosen_grad + d_middle + d_first + d_gate * router[...]).astype(BF16)
    grad_router = jnp.sum(d_gate * x, 0, keepdims=True)
    small = jnp.concatenate(
        [grad_router, grad_gain_one, grad_gain_two, jnp.zeros((EXTRA - 3, model), F32)], 0
    ).astype(BF16)
    body = tensor_size * types * per_shard * width
    for which, out in ((core, keep_ref), (1 - core, send_ref)):
        for c in range(pieces):
            for z in range(tensor_size):
                for t in range(types):
                    for h in range(per_shard):
                        source = (z * per_shard + h) * HD + c * width
                        start = ((z * types + t) * per_shard + h) * width
                        out[c, start : start + width, :] = grads[
                            2 * which + t, source : source + width, :
                        ]
            out[c, body : body + EXTRA, :] = small


def call(kernel, outs, args, scratch=(), flops=0, aliases=None):
    size = sum(a.size * a.dtype.itemsize for a in args) + sum(
        o.size * o.dtype.itemsize for o in outs
    )
    whole = pl.BlockSpec(memory_space=pltpu.VMEM)
    in_specs = [
        pl.BlockSpec(memory_space=pltpu.SMEM) if a.shape == (1,) else whole for a in args
    ]
    return pl.pallas_call(
        kernel,
        out_shape=outs,
        in_specs=in_specs,
        out_specs=[whole] * len(outs),
        scratch_shapes=scratch,
        input_output_aliases=aliases or {},
        compiler_params=pltpu.CompilerParams(vmem_limit_bytes=VMEM_LIMIT),
        cost_estimate=pl.CostEstimate(flops=flops, bytes_accessed=size, transcendentals=0),
    )(*args)


def local(
    dp_size,
    tensor_size,
    tokens,
    segment_ids,
    selected,
    w_router,
    gain_one,
    w_query,
    w_key,
    w_value,
    w_out,
    gain_two,
    w_up,
    w_down,
    grad_out,
):
    row_count, local_len, model = tokens.shape
    picks = selected.shape[1]
    full_len = segment_ids.shape[1]
    chips = dp_size // 2
    width = HD // chips
    per_shard = w_query.shape[1] // HD
    hidden_width = w_up.shape[1] // dp_size
    assert row_count == tensor_size and HD % chips == 0
    dp_index = lax.axis_index("dp")
    my_z = lax.axis_index("tensor")
    core, chip = dp_index % 2, dp_index // 2

    def to_core(values):
        return lax.ppermute(values, "dp", [(i, i ^ 1) for i in range(dp_size)])

    def to_chip(values, k):
        return lax.ppermute(values, "dp", [(i, i ^ (2 * k)) for i in range(dp_size)])

    def to_z(values, k):
        return lax.ppermute(values, "tensor", [(i, i ^ k) for i in range(tensor_size)])

    first = jnp.where(core == 0, w_query.T, w_value.T)
    second = jnp.where(core == 0, w_key.T, w_out)
    both = jnp.stack([first, second]).reshape(2, per_shard, chips, width, model)
    attn_mine = lax.dynamic_index_in_dim(both, chip, 2, keepdims=False)
    up_mine = lax.dynamic_slice_in_dim(w_up, dp_index * hidden_width, hidden_width, 1).T
    down_mine = lax.dynamic_slice_in_dim(w_down, dp_index * hidden_width, hidden_width, 0)
    ffn_mine = jnp.stack([up_mine, down_mine])

    attn_z = jnp.stack([attn_mine] + [to_z(attn_mine, k) for k in range(1, tensor_size)])
    ffn_z = jnp.stack([ffn_mine] + [to_z(ffn_mine, k) for k in range(1, tensor_size)])
    attn_own = [attn_z] + [to_chip(attn_z, k) for k in range(1, chips)]
    attn_oth = [to_core(piece) for piece in attn_own]
    ffn_own = [ffn_z] + [to_chip(ffn_z, k) for k in range(1, chips)]
    if width % 16:
        merge = lambda parts: jnp.stack(parts, 3).reshape(
            tensor_size, 2, per_shard, HD, model
        )
        attn_own, attn_oth = [merge(attn_own)], [merge(attn_oth)]
    step = 1
    while (hidden_width * step) % 16:
        step *= 2
    merged = [
        jnp.concatenate(ffn_own[i : i + step], 2) for i in range(0, chips, step)
    ]

    local_pos = my_z * local_len + jnp.arange(local_len, dtype=jnp.int32)
    hit = selected[:, :, None] == local_pos[None, None, :]
    hit_bf = hit.astype(BF16)

    def take(values):
        part = jnp.einsum("rkl,rld->rkd", hit_bf, values, preferred_element_type=F32)
        return lax.psum_scatter(part.astype(BF16), "tensor", scatter_dimension=0, tiled=True)[0]

    chosen = take(tokens)
    chosen_grad = take(grad_out)
    my_sel = lax.dynamic_index_in_dim(selected, my_z, 0, keepdims=False)
    my_seg = lax.dynamic_index_in_dim(segment_ids, my_z, 0, keepdims=False)
    full_pos = jnp.arange(full_len, dtype=jnp.int32)
    tags = jnp.sum(jnp.where(my_sel[:, None] == full_pos[None, :], my_seg[None, :], 0), 1)
    tag_col, tag_row = tags[:, None], tags[None, :]
    core_arr = core.reshape(1)
    g_one, g_two = gain_one[None, :], gain_two[None, :]
    router = w_router.astype(F32)[None, :]

    row_bf = jax.ShapeDtypeStruct((picks, model), BF16)
    row_f32 = jax.ShapeDtypeStruct((picks, model), F32)
    head_dims = per_shard * tensor_size * HD
    heads = per_shard * tensor_size
    table = pltpu.VMEM((4, head_dims, model), BF16)
    weights = attn_own + attn_oth
    q, k, v, mixed, lse, attended, normed_two, gate = call(
        functools.partial(attend_kernel, len(attn_own)),
        [row_bf] * 4
        + [jax.ShapeDtypeStruct((picks, heads), F32), row_f32, row_bf]
        + [jax.ShapeDtypeStruct((picks, 1), F32)],
        [core_arr, chosen, tag_col, tag_row, g_one, g_two, router] + weights,
        [table],
        flops=10 * picks * model * model,
    )

    d_branch = (gate * chosen_grad.astype(F32)).astype(BF16)
    n2_oth, db_oth = to_core(normed_two), to_core(d_branch)
    groups = 2 if len(merged) % 2 == 0 else 1
    per_call = len(merged) // groups
    acc, grad_pieces = [], []
    for g in range(groups):
        mine = merged[g * per_call : (g + 1) * per_call]
        last = g == groups - 1
        pair = jax.ShapeDtypeStruct((2 * picks, model), F32)
        outs = [jax.ShapeDtypeStruct(p.shape, BF16) for p in mine] + (
            [row_f32, row_bf] * 2 if last else [pair] * 2
        )
        results = call(
            functools.partial(hidden_kernel, per_call, g == 0, last),
            outs,
            [normed_two, n2_oth, d_branch, db_oth] + mine + acc,
            flops=12 * 2 * picks * model * mine[0].shape[2] * tensor_size * per_call,
        )
        grad_pieces += results[:per_call]
        acc = list(results[per_call:])
    dn_own, dn_send, br_own, br_send = acc
    if step > 1:
        grad_pieces = [
            p[:, :, i * hidden_width : (i + 1) * hidden_width]
            for p in grad_pieces
            for i in range(step)
        ]
    dn_recv, br_recv = to_core(dn_send), to_core(br_send)

    def total(parts):
        return sum(p.astype(F32) for p in parts).astype(BF16)

    ffn_sum = total([grad_pieces[0]] + [to_chip(grad_pieces[k], k) for k in range(1, chips)])
    ffn_sum = total([ffn_sum[0]] + [to_z(ffn_sum[k], k) for k in range(1, tensor_size)])
    ffn_all = lax.all_gather(ffn_sum, "dp", axis=0, tiled=False)
    grad_up = ffn_all[:, 0].reshape(w_up.shape[1], model).astype(F32).T
    grad_down = ffn_all[:, 1].reshape(w_up.shape[1], model).astype(F32)

    branch = br_own + br_recv.astype(F32)
    updated = (chosen.astype(F32) + gate * (attended + branch)).astype(BF16)
    updated_all = lax.all_gather(updated, "tensor", axis=0, tiled=False)

    covered = jnp.any(hit, axis=1)[:, :, None]

    def place(values, initial):
        placed = jnp.einsum("rkl,rkd->rld", hit_bf, values, preferred_element_type=F32)
        return jnp.where(covered, placed.astype(BF16), initial)

    layer_out = place(updated_all, tokens)

    piece_count = len(attn_own)
    body = tensor_size * 2 * per_shard * (HD // piece_count)
    packed = jax.ShapeDtypeStruct((piece_count, body + EXTRA, model), BF16)
    keep, send, d_chosen = call(
        functools.partial(back_kernel, piece_count),
        [packed, packed, row_bf],
        [core_arr, chosen, chosen_grad, gate, attended, br_own, br_recv, dn_own, dn_recv]
        + [q, k, v, mixed, lse, tag_col, tag_row, g_one, g_two, router]
        + weights,
        [table, table] + [pltpu.VMEM((picks, head_dims), BF16)] * 3,
        flops=20 * picks * model * model,
    )
    grad_all = lax.all_gather(d_chosen, "tensor", axis=0, tiled=False)
    grad_tokens = place(grad_all, grad_out)

    recv = to_core(send)
    if piece_count == chips:
        halves = [total([keep[k], recv[k]]) for k in range(chips)]
    else:
        both = total([keep[0], recv[0]])
        blocks = both[:body].reshape(-1, chips, width, model)
        halves = [
            jnp.concatenate([blocks[:, k].reshape(-1, model), both[body:]], 0)
            for k in range(chips)
        ]
    attn_sum = total([halves[0]] + [to_chip(halves[k], k) for k in range(1, chips)])
    part = 2 * per_shard * width
    shards = [
        jnp.concatenate(
            [attn_sum[k * part : (k + 1) * part], attn_sum[tensor_size * part :]], 0
        )
        for k in range(tensor_size)
    ]
    attn_sum = total([shards[0]] + [to_z(shards[k], k) for k in range(1, tensor_size)])
    small = attn_sum[part:].astype(F32)
    attn_all = lax.all_gather(attn_sum[:part], "dp", axis=0, tiled=False)
    attn_all = attn_all.reshape(chips, 2, 2, per_shard, width, model).transpose(1, 2, 3, 0, 4, 5)
    attn_all = attn_all.reshape(4, per_shard * HD, model).astype(F32)
    return (
        layer_out,
        grad_tokens,
        small[0],
        small[1],
        attn_all[0].T,
        attn_all[1].T,
        attn_all[2].T,
        attn_all[3],
        small[2],
        grad_up,
        grad_down,
    )


def solution(mesh):
    placed = (
        P("dp", "tensor", None),
        P("dp", None),
        P("dp", None),
        P(),
        P(),
        P(None, "tensor"),
        P(None, "tensor"),
        P(None, "tensor"),
        P("tensor", None),
        P(),
        P(None, "tensor"),
        P("tensor", None),
        P("dp", "tensor", None),
    )
    return jax.shard_map(
        functools.partial(local, mesh.shape["dp"], mesh.shape["tensor"]),
        mesh=mesh,
        in_specs=placed,
        out_specs=(
            P("dp", "tensor", None),
            P("dp", "tensor", None),
            P(),
            P(),
            P(None, "tensor"),
            P(None, "tensor"),
            P(None, "tensor"),
            P("tensor", None),
            P(),
            P(None, "tensor"),
            P("tensor", None),
        ),
        check_vma=False,
    )
```

time: 895 us -> 378 us (0.42)
  waiting for transfers between devices: 704 us -> 200 us
  starting transfers between devices: 0.88 us -> 61.8 us
  matrix products: 73.5 us -> 17.1 us
  Pallas kernels: 0 us -> 39 us
  blocking collectives: 23.8 us -> 0 us
  local copies, waits for them, and re-layouts: 39.5 us -> 26.6 us
  other arithmetic: 30.6 us -> 17.8 us
    all_gather x2 -> x4, waiting for transfers between devices: 399 us -> 8.63 us  [the longest x1 8.61 us: local(): attn_all = lax.all_gather(attn_sum[:part], 'dp', axis=0, tiled=False)]
    psum x4 -> x0, waiting for transfers between devices: 304 us -> none  [the longest x1 117 us: local(): lax.psum(branch_part.astype(jnp.bfloat16), 'tensor').astype(jnp.float32)]
    ppermute x0 -> x33, waiting for transfers between devices: none -> 191 us  [the longest x12 102 us: to_chip(): return lax.ppermute(values, 'dp', [(i, i ^ 2 * k) for i in range(dp_size)])]
    ppermute x0 -> x33, starting transfers between devices: none -> 61.4 us  [the longest x12 43.4 us: to_z(): lax.ppermute(values, 'tensor', [(i, i ^ k) for i in range(tensor_size)])]
    dot_general x38 -> x4, matrix products: 73.5 us -> 17.1 us  [the longest x2 8.75 us: place(): jnp.einsum('rkl,rkd->rld', hit_bf, values, preferred_element_type=F32)]
    pallas_call x0 -> x4, Pallas kernels: none -> 39 us  [call(): pl.pallas_call(kernel, out_shape=outs, in_specs=in_specs, out_specs=[whol...]
    psum x1 -> x0, blocking collectives: 23.8 us -> none  [local(): lax.psum((grad_router, grad_gain_one, grad_query, grad_key, grad_value, g...]
    reduce_sum x6 -> x1, other arithmetic: 14.8 us -> 0.41 us  [local(): jnp.sum(jnp.where(my_sel[:, None] == full_pos[None, :], my_seg[None, :],...]
  transfers between devices with their start and end apart: 6 -> 39, of which waited for: 6 -> 20; matrix products, arithmetic and copies ran while one was open for 10% -> 10% of each run, Pallas kernels for 0% -> 4%
where the time goes in v1:
time: 378 us; the launch traced here: 377 us
  waiting for transfers between devices  200 us (53%)
  starting transfers between devices  61.8 us (16%)
  Pallas kernels  39 us (10%)
  local copies, waits for them, and re-layouts  26.6 us (7%)
  other arithmetic  17.8 us (5%)
  matrix products  17.1 us (5%)
  between operations  14.7 us (4%)
    ppermute x12, waiting for transfers between devices, to_chip(): return lax.ppermute(values, 'dp', [(i, i ^ 2 * k) for i in range(dp_size)])  102 us
    ppermute x12, waiting for transfers between devices, to_z(): lax.ppermute(values, 'tensor', [(i, i ^ k) for i in range(tensor_size)])  87.9 us
    ppermute x12, starting transfers between devices, to_z(): lax.ppermute(values, 'tensor', [(i, i ^ k) for i in range(tensor_size)])  43.4 us
    pallas_call x4, Pallas kernels, call(): pl.pallas_call(kernel, out_shape=outs, in_specs=in_specs, out_specs=[whol...  39 us
    unnamed x92, local copies, waits for them, and re-layouts  17.1 us
    ppermute x12, starting transfers between devices, to_chip(): return lax.ppermute(values, 'dp', [(i, i ^ 2 * k) for i in range(dp_size)])  15.8 us
    dot_general x2, matrix products, place(): jnp.einsum('rkl,rkd->rld', hit_bf, values, preferred_element_type=F32)  8.75 us
    all_gather x1, waiting for transfers between devices, local(): attn_all = lax.all_gather(attn_sum[:part], 'dp', axis=0, tiled=False)  8.61 us
  transfers between devices with their start and end apart: 39, of which 20 were waited for; matrix products, arithmetic and copies ran while one was open for 10% of the time, Pallas kernels for 4%

profile of v1, /device:TPU:0, one launch (start us, length us, event | category | flops | bytes accessed | tf_op | source)
XLA Modules:
  0.0 377.1 jit_solution(16400579802131940740)
XLA Ops:
  7.3 4.2 %fusion.12 = bf16[4,256,768]{2,1,0:T(8,128)(2,1)} fusion(bf16[4,512,768]{2,1,0:T(8,128)(2,1)} %param.13, s32[4,256]{1,0:T(4,128)} %param.15, s32[512]{0:T(512)S(1)} %iota_add_fusion), kind=kOutput, calls=%fused_computation.16 | convolution fusion | flops 806617088 | bytes 4724736 | tf_op jit(solution)/shard_map/rkl,rld->rkd/dot_general | solution.py:310
  12.2 4.1 %fusion.15 = bf16[4,256,768]{2,1,0:T(8,128)(2,1)} fusion(bf16[4,512,768]{2,1,0:T(8,128)(2,1)} %param.25, s32[4,256]{1,0:T(4,128)S(1)} %copy-done.43, s32[512]{0:T(512)S(1)} %iota_add_fusion), kind=kOutput, calls=%fused_computation.17 | convolution fusion | flops 806617088 | bytes 4724736 | tf_op jit(solution)/shard_map/rkl,rld->rkd/dot_general | solution.py:310
  17.6 3.1 collective-permute-start
  20.7 2.6 collective-permute-start.1
  23.6 0.9 dynamic-slice_bitcast_fusion
  24.5 7.6 %collective-permute-done = bf16[2,3,16,768]{3,2,1,0:T(8,128)(2,1)S(1)} collective-permute-done((bf16[2,3,16,768]{3,2,1,0:T(8,128)(2,1)S(1)}, bf16[2,3,16,768]{3,2,1,0:T(8,128)(2,1)S(1)}, u32[]{:S(2)}, u32[]{:S(2)}) %collective-permute-start) | collective-permute-done | bytes 147488 | tf_op jit(solution)/shard_map/ppermute | solution.py:278
  32.1 8.7 %collective-permute-done.1 = bf16[2,3,16,768]{3,2,1,0:T(8,128)(2,1)S(1)} collective-permute-done((bf16[2,3,16,768]{3,2,1,0:T(8,128)(2,1)S(1)}, bf16[2,3,16,768]{3,2,1,0:T(8,128)(2,1)S(1)}, u32[]{:S(2)}, u32[]{:S(2)}) %collective-permute-start.1) | collective-permute-done | bytes 147488 | tf_op jit(solution)/shard_map/ppermute | solution.py:278
  40.8 1.8 collective-permute-done.2
  42.8 1.6 collective-permute-start.3
  45.1 1.5 collective-permute-start.4
  47.1 11.6 %collective-permute-start.12 = (bf16[2,96,768]{2,1,0:T(8,128)(2,1)S(1)}, bf16[2,96,768]{2,1,0:T(8,128)(2,1)S(1)}, u32[]{:S(2)}, u32[]{:S(2)}) collective-permute-start(bf16[2,96,768]{2,1,0:T(8,128)(2,1)S(1)} %get-tuple-element.116), channel_id=1, source_target_pairs={{0,1},{1,0},{2,3},{3,2},{4,5},{5,4},{6,7},{7,6},{8,9},{9,8},{10,11... | collective-permute-start | bytes 884744 | tf_op jit(solution)/shard_map/ppermute | solution.py:278
  58.7 0.9 collective-permute-start.13
  59.5 11.1 %collective-permute-done.12 = bf16[2,96,768]{2,1,0:T(8,128)(2,1)S(1)} collective-permute-done((bf16[2,96,768]{2,1,0:T(8,128)(2,1)S(1)}, bf16[2,96,768]{2,1,0:T(8,128)(2,1)S(1)}, u32[]{:S(2)}, u32[]{:S(2)}) %collective-permute-start.12) | collective-permute-done | bytes 294944 | tf_op jit(solution)/shard_map/ppermute | solution.py:278
  70.7 13.8 %collective-permute-done.13 = bf16[2,96,768]{2,1,0:T(8,128)(2,1)S(1)} collective-permute-done((bf16[2,96,768]{2,1,0:T(8,128)(2,1)S(1)}, bf16[2,96,768]{2,1,0:T(8,128)(2,1)S(1)}, u32[]{:S(2)}, u32[]{:S(2)}) %collective-permute-start.13) | collective-permute-done | bytes 294944 | tf_op jit(solution)/shard_map/ppermute | solution.py:278
  85.6 2.4 collective-permute-done.14
  88.7 1.4 pad_maximum_fusion.refs_0_
  90.1 3.6 collective-permute-start.17
  96.0 1.6 collective-permute-start.15
  100.3 1.0 copy-done.4
  101.3 1.1 copy-done.19
  102.3 8.0 %shard_map.212 = (bf16[256,768]{1,0:T(8,128)(2,1)S(1)}, bf16[256,768]{1,0:T(8,128)(2,1)S(1)}, bf16[256,768]{1,0:T(8,128)(2,1)S(1)}, bf16[256,768]{1,0:T(8,128)(2...) custom-call(s32[1]{0:T(128)} %bitcast.1.core_ref, ...), custom_call_target="tpu_custom_call" | custom-call | flops 1509949440 | bytes 7888900 | tf_op jit(solution)/shard_map/pallas_call | solution.py:230
  114.2 1.2 multiply_convert_fusion.db_own
  116.0 4.5 %collective-permute-done.17.refs_1_ = bf16[4,2,96,768]{3,2,1,0:T(8,128)(2,1)} collective-permute-done((bf16[4,2,96,768]{3,2,1,0:T(8,128)(2,1)S(1)}, bf16[4,2,96,768]{3,2,1,0:T(8,128)(2,1)}, u32[]{:S(2)}, u32[]{:S(2)}) %collective-permute-start.17) | collective-permute-done | bytes 1179680 | tf_op jit(solution)/shard_map/ppermute | solution.py:275
  120.6 1.0 copy-done.21
  121.6 7.8 %shard_map.213 = (bf16[4,2,96,768]{3,2,1,0:T(8,128)(2,1)S(1)}, bf16[4,2,96,768]{3,2,1,0:T(8,128)(2,1)S(1)}, f32[512,768]{1,0:T(8,128)}, f32[512,768]{1,0:T(8,128)}) custom-call(bf16[256,768]{1,0:T(8,128)(2,1)S(1)} %copy-done.21, bf16[256,768]{1,0:T(8,128)(2,1)S(1)} %collective-permute-done.10.n2_oth, bf16[256,768]{1,0:T(8,128)(2,1)S(1)} %multiply_convert_fusion.db_own, ...), custom_call_target="tpu_custom_call" | custom-call | flops 3623878656 | bytes 9437184 | tf_op jit(solution)/shard_map/pallas_call | solution.py:230
  129.3 1.0 copy-done.12
  130.4 18.7 %collective-permute-done.15.refs_0_ = bf16[4,2,96,768]{3,2,1,0:T(8,128)(2,1)} collective-permute-done((bf16[4,2,96,768]{3,2,1,0:T(8,128)(2,1)S(1)}, bf16[4,2,96,768]{3,2,1,0:T(8,128)(2,1)}, u32[]{:S(2)}, u32[]{:S(2)}) %collective-permute-start.15) | collective-permute-done | bytes 1179680 | tf_op jit(solution)/shard_map/ppermute | solution.py:275
  149.1 9.2 %shard_map.214 = (bf16[4,2,96,768]{3,2,1,0:T(8,128)(2,1)S(1)}, bf16[4,2,96,768]{3,2,1,0:T(8,128)(2,1)}, f32[256,768]{1,0:T(8,128)S(1)}, bf16[256,768]{1,0:T(8,12...) custom-call(bf16[256,768]{1,0:T(8,128)(2,1)S(1)} %copy-done.22, ...), custom_call_target="tpu_custom_call" | custom-call | flops 3623878656 | bytes 11796480 | tf_op jit(solution)/shard_map/pallas_call | solution.py:230
  158.4 0.9 copy-done.2
  159.2 1.0 copy-done.13
  160.2 0.9 copy-done.31
  161.6 1.2 collective-permute-done.18.br_recv
  163.5 14.0 %shard_map.215 = (bf16[4,400,768]{2,1,0:T(8,128)(2,1)}, bf16[4,400,768]{2,1,0:T(8,128)(2,1)}, bf16[256,768]{1,0:T(8,128)(2,1)S(1)}) custom-call(s32[1]{0:T(128)} %bitcast.1.core_ref, bf16[256,768]{1,0:T(8,128)(2,1)S(1)} %bitcast.90, bf16[256,768]{1,0:T(8,128)(2,1)S(1)} %bitcast.91, f32[256,1]{1,0:T(8,128)S(1)} %copy-done.11, ...), custom_call_target="tpu_custom_call" | custom-call | flops 3019898880 | bytes 15556612 | tf_op jit(solution)/shard_map/pallas_call | solution.py:230
  178.3 1.7 collective-permute-start.28
  180.1 1.7 collective-permute-start.27
  181.8 2.1 add_convert_fusion.5
  184.0 48.0 %collective-permute-done.28 = bf16[4,2,96,768]{3,2,1,0:T(8,128)(2,1)} collective-permute-done((bf16[4,2,96,768]{3,2,1,0:T(8,128)(2,1)}, bf16[4,2,96,768]{3,2,1,0:T(8,128)(2,1)}, u32[]{:S(2)}, u32[]{:S(2)}) %collective-permute-start.28) | collective-permute-done | bytes 1179680 | tf_op jit(solution)/shard_map/ppermute | solution.py:275
  232.0 1.2 collective-permute-done.27
  233.2 2.7 add_convert_fusion
  236.0 12.7 %collective-permute-start.30 = (bf16[2,96,768]{2,1,0:T(8,128)(2,1)S(1)}, bf16[2,96,768]{2,1,0:T(8,128)(2,1)S(1)}, u32[]{:S(2)}, u32[]{:S(2)}) collective-permute-start(bf16[2,96,768]{2,1,0:T(8,128)(2,1)S(1)} %get-tuple-element.109), channel_id=1, source_target_pairs={{0,1},{1,0},{2,3},{3,2},{4,5},{5,4},{6,7},{7,6},{8,9},{9,8},{10,11... | collective-permute-start | bytes 884744 | tf_op jit(solution)/shard_map/ppermute | solution.py:278
  248.7 0.9 collective-permute-start.31
  249.6 1.5 collective-permute-start.32
  251.2 23.4 %collective-permute-done.30 = bf16[2,96,768]{2,1,0:T(8,128)(2,1)S(1)} collective-permute-done((bf16[2,96,768]{2,1,0:T(8,128)(2,1)S(1)}, bf16[2,96,768]{2,1,0:T(8,128)(2,1)S(1)}, u32[]{:S(2)}, u32[]{:S(2)}) %collective-permute-start.30) | collective-permute-done | bytes 294944 | tf_op jit(solution)/shard_map/ppermute | solution.py:278
  274.6 2.2 collective-permute-done.31
  276.8 6.4 %collective-permute-done.32 = bf16[2,96,768]{2,1,0:T(8,128)(2,1)S(1)} collective-permute-done((bf16[2,96,768]{2,1,0:T(8,128)(2,1)S(1)}, bf16[2,96,768]{2,1,0:T(8,128)(2,1)S(1)}, u32[]{:S(2)}, u32[]{:S(2)}) %collective-permute-start.32) | collective-permute-done | bytes 294944 | tf_op jit(solution)/shard_map/ppermute | solution.py:278
  283.2 0.9 fusion.35
  284.2 2.4 fusion.30
  286.6 1.5 collective-permute-start.21
  288.1 1.5 collective-permute-start.22
  290.1 16.5 %collective-permute-done.21 = bf16[400,768]{1,0:T(8,128)(2,1)S(1)} collective-permute-done((bf16[400,768]{1,0:T(8,128)(2,1)S(1)}, bf16[400,768]{1,0:T(8,128)(2,1)S(1)}, u32[]{:S(2)}, u32[]{:S(2)}) %collective-permute-start.21) | collective-permute-done | bytes 614432 | tf_op jit(solution)/shard_map/ppermute | solution.py:275
  306.6 12.7 %collective-permute-done.22 = bf16[400,768]{1,0:T(8,128)(2,1)S(1)} collective-permute-done((bf16[400,768]{1,0:T(8,128)(2,1)S(1)}, bf16[400,768]{1,0:T(8,128)(2,1)S(1)}, u32[]{:S(2)}, u32[]{:S(2)}) %collective-permute-start.22) | collective-permute-done | bytes 614432 | tf_op jit(solution)/shard_map/ppermute | solution.py:275
  319.4 1.7 fusion.20
  321.2 7.5 %collective-permute-start.24 = (bf16[112,768]{1,0:T(8,128)(2,1)S(1)}, bf16[112,768]{1,0:T(8,128)(2,1)S(1)}, u32[]{:S(2)}, u32[]{:S(2)}) collective-permute-start(bf16[112,768]{1,0:T(8,128)(2,1)S(1)} %get-tuple-element.117), channel_id=1, source_target_pairs={{0,1},{1,0},{2,3},{3,2},{4,5},{5,4},{6,7},{7,6},{8,9},{9,8},{10,11... | collective-permute-start | bytes 516104 | tf_op jit(solution)/shard_map/ppermute | solution.py:278
  328.7 2.4 collective-permute-start.26
  331.2 4.5 %collective-permute-done.24 = bf16[112,768]{1,0:T(8,128)(2,1)S(1)} collective-permute-done((bf16[112,768]{1,0:T(8,128)(2,1)S(1)}, bf16[112,768]{1,0:T(8,128)(2,1)S(1)}, u32[]{:S(2)}, u32[]{:S(2)}) %collective-permute-start.24) | collective-permute-done | bytes 172064 | tf_op jit(solution)/shard_map/ppermute | solution.py:278
  335.7 5.8 %collective-permute-done.25 = bf16[112,768]{1,0:T(8,128)(2,1)S(1)} collective-permute-done((bf16[112,768]{1,0:T(8,128)(2,1)S(1)}, bf16[112,768]{1,0:T(8,128)(2,1)S(1)}, u32[]{:S(2)}, u32[]{:S(2)}) %collective-permute-start.25) | collective-permute-done | bytes 172064 | tf_op jit(solution)/shard_map/ppermute | solution.py:278
  342.8 4.4 %convert_select_fusion = bf16[4,512,768]{2,1,0:T(8,128)(2,1)} fusion(bf16[4,512,768]{2,1,0:T(8,128)(2,1)} %param.25, pred[4,512]{1,0:T(4,128)(4,1)S(1)} %compare_reduce_fusion, bf16[4,256,768]{2,1,0:T(8,128)(2,1)} %bitcast.113, s32[4,256]{1,0:T(4,128)S(1)} %copy-done.44, s32[512]{0:T(512)S(1)} %copy-done.42), kind=kOutput, calls=%fused_computation.9 | convolution fusion | flops 808976384 | bytes 7872512 | tf_op jit(solution)/shard_map/rkl,rkd->rld/dot_general | solution.py:385
  347.2 4.4 %convert_select_fusion.1 = bf16[4,512,768]{2,1,0:T(8,128)(2,1)} fusion(bf16[4,512,768]{2,1,0:T(8,128)(2,1)} %param.13, pred[4,512]{1,0:T(4,128)(4,1)S(1)} %compare_reduce_fusion, bf16[4,256,768]{2,1,0:T(8,128)(2,1)} %bitcast.114, s32[4,256]{1,0:T(4,128)S(1)} %copy-done.44, s32[512]{0:T(512)S(1)} %copy-done.42), kind=kOutput, calls=%fused_computation.10 | convolution fusion | flops 808976384 | bytes 7872512 | tf_op jit(solution)/shard_map/rkl,rkd->rld/dot_general | solution.py:385
  352.2 1.8 fusion.38
  354.0 1.9 convert_bitcast_fusion
  355.9 1.9 copy.67
  357.9 8.6 %all-gather.13.cloned.1.call-done = bf16[768,768]{1,0:T(8,128)(2,1)} async-done(((bf16[96,768]{1,0:T(8,128)(2,1)}), bf16[768,768]{1,0:T(8,128)(2,1)}) %all-gather.13.cloned.1.call-update) | async-done | bytes 1179664 | tf_op jit(solution)/shard_map/all_gather | solution.py:425
  366.5 1.6 convert_bitcast_fusion.1
  368.3 1.4 slice_bitcast_fusion
  (158 shorter events, 20.3 us)
Async XLA Ops:
  7.2 16.1 %copy-start = (bf16[768,768]{1,0:T(8,128)(2,1)S(1)}, bf16[768,768]{1,0:T(8,128)(2,1)}, u32[]{:S(2)}) copy-start(bf16[768,768]{1,0:T(8,128)(2,1)} %param.23) | copy-start | bytes 3538948
  7.2 93.1 %reduce-scatter.3.cloned.1.call-start = ((), (), s32[]{:S(2)}) async-start(), calls=%async_computation.2 | async-start | bytes 1966080 | tf_op jit(solution)/shard_map/reduce_scatter | solution.py:311
  7.3 4.3 %copy-start.41 = (s32[512]{0:T(512)}, s32[512]{0:T(512)S(1)}, u32[]{:S(2)}) copy-start(s32[512]{0:T(512)S(1)} %iota_add_fusion) | copy-start | bytes 6148
  11.5 102.7 %reduce-scatter.5.cloned.1.call-start = ((), (), s32[]{:S(2)}) async-start(), calls=%async_computation.3 | async-start | bytes 1966080 | tf_op jit(solution)/shard_map/reduce_scatter | solution.py:311
  16.4 326.5 %all-gather.11.cloned.1.call-start = ((), (), s32[]{:S(2)}) async-start(), calls=%async_computation.5 | async-start | bytes 1966080 | tf_op jit(solution)/shard_map/all_gather | solution.py:402
  17.6 14.5 %collective-permute-start = (bf16[2,3,16,768]{3,2,1,0:T(8,128)(2,1)S(1)}, bf16[2,3,16,768]{3,2,1,0:T(8,128)(2,1)S(1)}, u32[]{:S(2)}, u32[]{:S(2)}) collective-permute-start(bf16[2,3,16,768]{3,2,1,0:T(8,128)(2,1)S(1)} %bitcast.100), channel_id=1, source_target_pairs={{0,1},{1,0},{2,3},{3,2},{4,5},{5,4},{6,7},{7,6},{8,9},{9,8},{10,11... | collective-permute-start | bytes 442376 | tf_op jit(solution)/shard_map/ppermute | solution.py:278
  20.7 20.1 %collective-permute-start.1 = (bf16[2,3,16,768]{3,2,1,0:T(8,128)(2,1)S(1)}, bf16[2,3,16,768]{3,2,1,0:T(8,128)(2,1)S(1)}, u32[]{:S(2)}, u32[]{:S(2)}) collective-permute-start(bf16[2,3,16,768]{3,2,1,0:T(8,128)(2,1)S(1)} %bitcast.101), channel_id=1, source_target_pairs={{0,2},{1,3},{2,0},{3,1},{4,6},{5,7},{6,4},{7,5},{8,10},{9,11},{10,... | collective-permute-start | bytes 442376 | tf_op jit(solution)/shard_map/ppermute | solution.py:278
  23.3 19.4 %collective-permute-start.2 = (bf16[2,3,16,768]{3,2,1,0:T(8,128)(2,1)S(1)}, bf16[2,3,16,768]{3,2,1,0:T(8,128)(2,1)S(1)}, u32[]{:S(2)}, u32[]{:S(2)}) collective-permute-start(bf16[2,3,16,768]{3,2,1,0:T(8,128)(2,1)S(1)} %bitcast.102), channel_id=1, source_target_pairs={{0,3},{1,2},{2,1},{3,0},{4,7},{5,6},{6,5},{7,4},{8,11},{9,10},{10,... | collective-permute-start | bytes 442376 | tf_op jit(solution)/shard_map/ppermute | solution.py:278
  42.8 41.8 %collective-permute-start.3 = (bf16[4,2,3,16,768]{4,3,2,1,0:T(8,128)(2,1)S(1)}, bf16[4,2,3,16,768]{4,3,2,1,0:T(8,128)(2,1)S(1)}, u32[]{:S(2)}, u32[]{:S(2)}) collective-permute-start(bf16[4,2,3,16,768]{4,3,2,1,0:T(8,128)(2,1)S(1)} %pad_maximum_fusion.1.refs_0_), channel_id=1, source_target_pairs={{0,8},{4,12},{8,0},{12,4},{16,24},{20,28},{24,16},{28,20},{1,9},{5... | collective-permute-start | bytes 1769480 | tf_op jit(solution)/shard_map/ppermute | solution.py:275
  45.1 40.0 %collective-permute-start.4 = (bf16[4,2,3,16,768]{4,3,2,1,0:T(8,128)(2,1)S(1)}, bf16[4,2,3,16,768]{4,3,2,1,0:T(8,128)(2,1)S(1)}, u32[]{:S(2)}, u32[]{:S(2)}) collective-permute-start(bf16[4,2,3,16,768]{4,3,2,1,0:T(8,128)(2,1)S(1)} %pad_maximum_fusion.1.refs_0_), channel_id=1, source_target_pairs={{0,16},{4,20},{8,24},{12,28},{16,0},{20,4},{24,8},{28,12},{1,17},{... | collective-permute-start | bytes 1769480 | tf_op jit(solution)/shard_map/ppermute | solution.py:275
  46.6 38.6 %collective-permute-start.5 = (bf16[4,2,3,16,768]{4,3,2,1,0:T(8,128)(2,1)S(1)}, bf16[4,2,3,16,768]{4,3,2,1,0:T(8,128)(2,1)}, u32[]{:S(2)}, u32[]{:S(2)}) collective-permute-start(bf16[4,2,3,16,768]{4,3,2,1,0:T(8,128)(2,1)S(1)} %pad_maximum_fusion.1.refs_0_), channel_id=1, source_target_pairs={{0,24},{4,28},{8,16},{12,20},{16,8},{20,12},{24,0},{28,4},{1,25},{... | collective-permute-start | bytes 1769480 | tf_op jit(solution)/shard_map/ppermute | solution.py:275
  47.1 23.5 %collective-permute-start.12 = (bf16[2,96,768]{2,1,0:T(8,128)(2,1)S(1)}, bf16[2,96,768]{2,1,0:T(8,128)(2,1)S(1)}, u32[]{:S(2)}, u32[]{:S(2)}) collective-permute-start(bf16[2,96,768]{2,1,0:T(8,128)(2,1)S(1)} %get-tuple-element.116), channel_id=1, source_target_pairs={{0,1},{1,0},{2,3},{3,2},{4,5},{5,4},{6,7},{7,6},{8,9},{9,8},{10,11... | collective-permute-start | bytes 884744 | tf_op jit(solution)/shard_map/ppermute | solution.py:278
  58.7 25.9 %collective-permute-start.13 = (bf16[2,96,768]{2,1,0:T(8,128)(2,1)S(1)}, bf16[2,96,768]{2,1,0:T(8,128)(2,1)S(1)}, u32[]{:S(2)}, u32[]{:S(2)}) collective-permute-start(bf16[2,96,768]{2,1,0:T(8,128)(2,1)S(1)} %get-tuple-element.116), channel_id=1, source_target_pairs={{0,2},{1,3},{2,0},{3,1},{4,6},{5,7},{6,4},{7,5},{8,10},{9,11},{10,... | collective-permute-start | bytes 884744 | tf_op jit(solution)/shard_map/ppermute | solution.py:278
  70.6 17.4 %copy-start.34 = (bf16[2,96,768]{2,1,0:T(8,128)(2,1)}, bf16[2,96,768]{2,1,0:T(8,128)(2,1)S(1)}, u32[]{:S(2)}) copy-start(bf16[2,96,768]{2,1,0:T(8,128)(2,1)S(1)} %collective-permute-done.12) | copy-start | bytes 884740
  70.6 17.4 %collective-permute-start.14 = (bf16[2,96,768]{2,1,0:T(8,128)(2,1)S(1)}, bf16[2,96,768]{2,1,0:T(8,128)(2,1)S(1)}, u32[]{:S(2)}, u32[]{:S(2)}) collective-permute-start(bf16[2,96,768]{2,1,0:T(8,128)(2,1)S(1)} %get-tuple-element.116), channel_id=1, source_target_pairs={{0,3},{1,2},{2,1},{3,0},{4,7},{5,6},{6,5},{7,4},{8,11},{9,10},{10,... | collective-permute-start | bytes 884744 | tf_op jit(solution)/shard_map/ppermute | solution.py:278
  84.6 3.4 copy-start.35
  84.6 10.6 %collective-permute-start.6 = (bf16[4,2,3,16,768]{4,3,2,1,0:T(8,128)(2,1)S(1)}, bf16[4,2,3,16,768]{4,3,2,1,0:T(8,128)(2,1)S(1)}, u32[]{:S(2)}, u32[]{:S(2)}) collective-permute-start(bf16[4,2,3,16,768]{4,3,2,1,0:T(8,128)(2,1)S(1)} %pad_maximum_fusion.1.refs_0_), channel_id=1, source_target_pairs={{0,4},{4,0},{8,12},{12,8},{16,20},{20,16},{24,28},{28,24},{1,5},{5... | collective-permute-start | bytes 1769480 | tf_op jit(solution)/shard_map/ppermute | solution.py:272
  84.6 25.8 %copy-start.14 = (bf16[4,2,3,16,768]{4,3,2,1,0:T(8,128)(2,1)}, bf16[4,2,3,16,768]{4,3,2,1,0:T(8,128)(2,1)S(1)}, u32[]{:S(2)}) copy-start(bf16[4,2,3,16,768]{4,3,2,1,0:T(8,128)(2,1)S(1)} %collective-permute-done.3.refs_1_) | copy-start | bytes 1769476
  84.6 13.0 %collective-permute-start.7 = (bf16[4,2,3,16,768]{4,3,2,1,0:T(8,128)(2,1)S(1)}, bf16[4,2,3,16,768]{4,3,2,1,0:T(8,128)(2,1)}, u32[]{:S(2)}, u32[]{:S(2)}) collective-permute-start(bf16[4,2,3,16,768]{4,3,2,1,0:T(8,128)(2,1)S(1)} %collective-permute-done.3.refs_1_), channel_id=1, source_target_pairs={{0,4},{4,0},{8,12},{12,8},{16,20},{20,16},{24,28},{28,24},{1,5},{5... | collective-permute-start | bytes 1769480 | tf_op jit(solution)/shard_map/ppermute | solution.py:272
  85.1 25.3 %copy-start.16 = (bf16[4,2,3,16,768]{4,3,2,1,0:T(8,128)(2,1)}, bf16[4,2,3,16,768]{4,3,2,1,0:T(8,128)(2,1)S(1)}, u32[]{:S(2)}) copy-start(bf16[4,2,3,16,768]{4,3,2,1,0:T(8,128)(2,1)S(1)} %collective-permute-done.4.refs_2_) | copy-start | bytes 1769476
  85.1 15.1 %collective-permute-start.8 = (bf16[4,2,3,16,768]{4,3,2,1,0:T(8,128)(2,1)S(1)}, bf16[4,2,3,16,768]{4,3,2,1,0:T(8,128)(2,1)}, u32[]{:S(2)}, u32[]{:S(2)}) collective-permute-start(bf16[4,2,3,16,768]{4,3,2,1,0:T(8,128)(2,1)S(1)} %collective-permute-done.4.refs_2_), channel_id=1, source_target_pairs={{0,4},{4,0},{8,12},{12,8},{16,20},{20,16},{24,28},{28,24},{1,5},{5... | collective-permute-start | bytes 1769480 | tf_op jit(solution)/shard_map/ppermute | solution.py:272
  85.2 15.1 %collective-permute-start.9 = (bf16[4,2,3,16,768]{4,3,2,1,0:T(8,128)(2,1)}, bf16[4,2,3,16,768]{4,3,2,1,0:T(8,128)(2,1)}, u32[]{:S(2)}, u32[]{:S(2)}) collective-permute-start(bf16[4,2,3,16,768]{4,3,2,1,0:T(8,128)(2,1)} %collective-permute-done.5.refs_3_), channel_id=1, source_target_pairs={{0,4},{4,0},{8,12},{12,8},{16,20},{20,16},{24,28},{28,24},{1,5},{5... | collective-permute-start | bytes 1769480 | tf_op jit(solution)/shard_map/ppermute | solution.py:272
  90.1 30.4 %collective-permute-start.17 = (bf16[4,2,96,768]{3,2,1,0:T(8,128)(2,1)S(1)}, bf16[4,2,96,768]{3,2,1,0:T(8,128)(2,1)}, u32[]{:S(2)}, u32[]{:S(2)}) collective-permute-start(bf16[4,2,96,768]{3,2,1,0:T(8,128)(2,1)S(1)} %pad_maximum_fusion.refs_0_), channel_id=1, source_target_pairs={{0,8},{4,12},{8,0},{12,4},{16,24},{20,28},{24,16},{28,20},{1,9},{5... | collective-permute-start | bytes 3538952 | tf_op jit(solution)/shard_map/ppermute | solution.py:275
  96.0 53.1 %collective-permute-start.15 = (bf16[4,2,96,768]{3,2,1,0:T(8,128)(2,1)S(1)}, bf16[4,2,96,768]{3,2,1,0:T(8,128)(2,1)}, u32[]{:S(2)}, u32[]{:S(2)}) collective-permute-start(bf16[4,2,96,768]{3,2,1,0:T(8,128)(2,1)S(1)} %pad_maximum_fusion.refs_0_), channel_id=1, source_target_pairs={{0,16},{4,20},{8,24},{12,28},{16,0},{20,4},{24,8},{28,12},{1,17},{... | collective-permute-start | bytes 3538952 | tf_op jit(solution)/shard_map/ppermute | solution.py:275
  97.6 51.5 %collective-permute-start.16 = (bf16[4,2,96,768]{3,2,1,0:T(8,128)(2,1)S(1)}, bf16[4,2,96,768]{3,2,1,0:T(8,128)(2,1)}, u32[]{:S(2)}, u32[]{:S(2)}) collective-permute-start(bf16[4,2,96,768]{3,2,1,0:T(8,128)(2,1)S(1)} %pad_maximum_fusion.refs_0_), channel_id=1, source_target_pairs={{0,24},{4,28},{8,16},{12,20},{16,8},{20,12},{24,0},{28,4},{1,25},{... | collective-permute-start | bytes 3538952 | tf_op jit(solution)/shard_map/ppermute | solution.py:275
  98.1 12.2 %copy-start.8 = (s32[256,1]{1,0:T(8,128)}, s32[256,1]{1,0:T(8,128)S(1)}, u32[]{:S(2)}) copy-start(s32[256,1]{1,0:T(8,128)S(1)} %copy.62.tag_col) | copy-start | bytes 3076
  114.1 6.5 %copy-start.10 = (f32[256,1]{1,0:T(8,128)}, f32[256,1]{1,0:T(8,128)S(1)}, u32[]{:S(2)}) copy-start(f32[256,1]{1,0:T(8,128)S(1)} %get-tuple-element.32.gate_ref) | copy-start | bytes 3076
  114.1 6.5 %copy-start.32 = (f32[256,12]{1,0:T(8,128)}, f32[256,12]{1,0:T(8,128)S(1)}, u32[]{:S(2)}) copy-start(f32[256,12]{1,0:T(8,128)S(1)} %get-tuple-element.45.lse_ref) | copy-start | bytes 36868
  114.2 34.8 %copy-start.22 = (bf16[256,768]{1,0:T(8,128)(2,1)S(1)}, bf16[256,768]{1,0:T(8,128)(2,1)}, u32[]{:S(2)}) copy-start(bf16[256,768]{1,0:T(8,128)(2,1)} %copy-done.20) | copy-start | bytes 1179652
  115.4 5.1 %collective-permute-start.11 = (bf16[256,768]{1,0:T(8,128)(2,1)S(1)}, bf16[256,768]{1,0:T(8,128)(2,1)S(1)}, u32[]{:S(2)}, u32[]{:S(2)}) collective-permute-start(bf16[256,768]{1,0:T(8,128)(2,1)S(1)} %multiply_convert_fusion.db_own), channel_id=1, source_target_pairs={{0,4},{4,0},{8,12},{12,8},{16,20},{20,16},{24,28},{28,24},{1,5},{5... | collective-permute-start | bytes 1179656 | tf_op jit(solution)/shard_map/ppermute | solution.py:272
  115.5 5.0 %collective-permute-start.10 = (bf16[256,768]{1,0:T(8,128)(2,1)}, bf16[256,768]{1,0:T(8,128)(2,1)S(1)}, u32[]{:S(2)}, u32[]{:S(2)}) collective-permute-start(bf16[256,768]{1,0:T(8,128)(2,1)} %copy-done.20), channel_id=1, source_target_pairs={{0,4},{4,0},{8,12},{12,8},{16,20},{20,16},{24,28},{28,24},{1,5},{5... | collective-permute-start | bytes 1179656 | tf_op jit(solution)/shard_map/ppermute | solution.py:272
  149.0 14.4 %copy-start.5 = (bf16[1,256,768]{2,1,0:T(8,128)(2,1)S(1)}, bf16[1,256,768]{2,1,0:T(8,128)(2,1)}, u32[]{:S(2)}) copy-start(bf16[1,256,768]{2,1,0:T(8,128)(2,1)} %reduce-scatter.3.cloned.1.call-done) | copy-start | bytes 1179652
  149.0 14.4 %copy-start.6 = (bf16[1,256,768]{2,1,0:T(8,128)(2,1)S(1)}, bf16[1,256,768]{2,1,0:T(8,128)(2,1)}, u32[]{:S(2)}) copy-start(bf16[1,256,768]{2,1,0:T(8,128)(2,1)} %reduce-scatter.5.cloned.1.call-done) | copy-start | bytes 1179652
  149.0 14.4 %copy-start.9 = (s32[256,1]{1,0:T(8,128)S(1)}, s32[256,1]{1,0:T(8,128)}, u32[]{:S(2)}) copy-start(s32[256,1]{1,0:T(8,128)} %copy-done.8) | copy-start | bytes 3076
  149.0 14.4 %copy-start.11 = (f32[256,1]{1,0:T(8,128)S(1)}, f32[256,1]{1,0:T(8,128)}, u32[]{:S(2)}) copy-start(f32[256,1]{1,0:T(8,128)} %copy-done.10) | copy-start | bytes 3076
  149.1 14.4 %copy-start.15 = (bf16[4,2,3,16,768]{4,3,2,1,0:T(8,128)(2,1)S(1)}, bf16[4,2,3,16,768]{4,3,2,1,0:T(8,128)(2,1)}, u32[]{:S(2)}) copy-start(bf16[4,2,3,16,768]{4,3,2,1,0:T(8,128)(2,1)} %copy-done.14) | copy-start | bytes 1769476
  149.1 14.4 %copy-start.17 = (bf16[4,2,3,16,768]{4,3,2,1,0:T(8,128)(2,1)S(1)}, bf16[4,2,3,16,768]{4,3,2,1,0:T(8,128)(2,1)}, u32[]{:S(2)}) copy-start(bf16[4,2,3,16,768]{4,3,2,1,0:T(8,128)(2,1)} %copy-done.16) | copy-start | bytes 1769476
  149.1 14.4 %copy-start.24 = (bf16[256,768]{1,0:T(8,128)(2,1)S(1)}, bf16[256,768]{1,0:T(8,128)(2,1)}, u32[]{:S(2)}) copy-start(bf16[256,768]{1,0:T(8,128)(2,1)} %copy-done.23) | copy-start | bytes 1179652
  149.1 14.4 %copy-start.26 = (bf16[256,768]{1,0:T(8,128)(2,1)S(1)}, bf16[256,768]{1,0:T(8,128)(2,1)}, u32[]{:S(2)}) copy-start(bf16[256,768]{1,0:T(8,128)(2,1)} %copy-done.25) | copy-start | bytes 1179652
  149.1 14.4 %copy-start.28 = (bf16[256,768]{1,0:T(8,128)(2,1)S(1)}, bf16[256,768]{1,0:T(8,128)(2,1)}, u32[]{:S(2)}) copy-start(bf16[256,768]{1,0:T(8,128)(2,1)} %copy-done.27) | copy-start | bytes 1179652
  149.1 14.4 %copy-start.30 = (bf16[256,768]{1,0:T(8,128)(2,1)S(1)}, bf16[256,768]{1,0:T(8,128)(2,1)}, u32[]{:S(2)}) copy-start(bf16[256,768]{1,0:T(8,128)(2,1)} %copy-done.29) | copy-start | bytes 1179652
  149.1 14.4 %copy-start.33 = (f32[256,12]{1,0:T(8,128)S(1)}, f32[256,12]{1,0:T(8,128)}, u32[]{:S(2)}) copy-start(f32[256,12]{1,0:T(8,128)} %copy-done.32) | copy-start | bytes 36868
  161.1 1.7 collective-permute-start.18
  161.1 2.3 collective-permute-start.19
  163.5 18.3 %copy-start.3 = (f32[256,768]{1,0:T(8,128)S(1)}, f32[256,768]{1,0:T(8,128)}, u32[]{:S(2)}) copy-start(f32[256,768]{1,0:T(8,128)} %copy-done.2) | copy-start | bytes 2359300
  178.2 169.0 %all-gather.9.cloned.1.call-start = ((), (), s32[]{:S(2)}) async-start(), calls=%async_computation.4 | async-start | bytes 1966080 | tf_op jit(solution)/shard_map/all_gather | solution.py:380
  178.3 53.7 %collective-permute-start.28 = (bf16[4,2,96,768]{3,2,1,0:T(8,128)(2,1)}, bf16[4,2,96,768]{3,2,1,0:T(8,128)(2,1)}, u32[]{:S(2)}, u32[]{:S(2)}) collective-permute-start(bf16[4,2,96,768]{3,2,1,0:T(8,128)(2,1)} %copy-done.13), channel_id=1, source_target_pairs={{0,16},{4,20},{8,24},{12,28},{16,0},{20,4},{24,8},{28,12},{1,17},{... | collective-permute-start | bytes 3538952 | tf_op jit(solution)/shard_map/ppermute | solution.py:275
  180.0 52.0 %collective-permute-start.29 = (bf16[4,2,96,768]{3,2,1,0:T(8,128)(2,1)}, bf16[4,2,96,768]{3,2,1,0:T(8,128)(2,1)}, u32[]{:S(2)}, u32[]{:S(2)}) collective-permute-start(bf16[4,2,96,768]{3,2,1,0:T(8,128)(2,1)} %get-tuple-element.52), channel_id=1, source_target_pairs={{0,24},{4,28},{8,16},{12,20},{16,8},{20,12},{24,0},{28,4},{1,25},{... | collective-permute-start | bytes 3538952 | tf_op jit(solution)/shard_map/ppermute | solution.py:275
  180.1 53.1 %collective-permute-start.27 = (bf16[4,2,96,768]{3,2,1,0:T(8,128)(2,1)}, bf16[4,2,96,768]{3,2,1,0:T(8,128)(2,1)}, u32[]{:S(2)}, u32[]{:S(2)}) collective-permute-start(bf16[4,2,96,768]{3,2,1,0:T(8,128)(2,1)} %copy-done.12), channel_id=1, source_target_pairs={{0,8},{4,12},{8,0},{12,4},{16,24},{20,28},{24,16},{28,20},{1,9},{5... | collective-permute-start | bytes 3538952 | tf_op jit(solution)/shard_map/ppermute | solution.py:275
  183.9 168.3 %all-gather.15.cloned.1.call-start = ((), (), s32[]{:S(2)}) async-start(), calls=%async_computation.7 | async-start | bytes 2654208 | tf_op jit(solution)/shard_map/all_gather | solution.py:374
  236.0 38.6 %collective-permute-start.30 = (bf16[2,96,768]{2,1,0:T(8,128)(2,1)S(1)}, bf16[2,96,768]{2,1,0:T(8,128)(2,1)S(1)}, u32[]{:S(2)}, u32[]{:S(2)}) collective-permute-start(bf16[2,96,768]{2,1,0:T(8,128)(2,1)S(1)} %get-tuple-element.109), channel_id=1, source_target_pairs={{0,1},{1,0},{2,3},{3,2},{4,5},{5,4},{6,7},{7,6},{8,9},{9,8},{10,11... | collective-permute-start | bytes 884744 | tf_op jit(solution)/shard_map/ppermute | solution.py:278
  248.7 28.1 %collective-permute-start.31 = (bf16[2,96,768]{2,1,0:T(8,128)(2,1)S(1)}, bf16[2,96,768]{2,1,0:T(8,128)(2,1)S(1)}, u32[]{:S(2)}, u32[]{:S(2)}) collective-permute-start(bf16[2,96,768]{2,1,0:T(8,128)(2,1)S(1)} %get-tuple-element.111), channel_id=1, source_target_pairs={{0,2},{1,3},{2,0},{3,1},{4,6},{5,7},{6,4},{7,5},{8,10},{9,11},{10,... | collective-permute-start | bytes 884744 | tf_op jit(solution)/shard_map/ppermute | solution.py:278
  249.6 33.6 %collective-permute-start.32 = (bf16[2,96,768]{2,1,0:T(8,128)(2,1)S(1)}, bf16[2,96,768]{2,1,0:T(8,128)(2,1)S(1)}, u32[]{:S(2)}, u32[]{:S(2)}) collective-permute-start(bf16[2,96,768]{2,1,0:T(8,128)(2,1)S(1)} %get-tuple-element.110), channel_id=1, source_target_pairs={{0,3},{1,2},{2,1},{3,0},{4,7},{5,6},{6,5},{7,4},{8,11},{9,10},{10,... | collective-permute-start | bytes 884744 | tf_op jit(solution)/shard_map/ppermute | solution.py:278
  251.2 33.0 %collective-permute-start.20 = (bf16[4,400,768]{2,1,0:T(8,128)(2,1)}, bf16[4,400,768]{2,1,0:T(8,128)(2,1)}, u32[]{:S(2)}, u32[]{:S(2)}) collective-permute-start(bf16[4,400,768]{2,1,0:T(8,128)(2,1)} %get-tuple-element.48), channel_id=1, source_target_pairs={{0,4},{4,0},{8,12},{12,8},{16,20},{20,16},{24,28},{28,24},{1,5},{5... | collective-permute-start | bytes 7372808 | tf_op jit(solution)/shard_map/ppermute | solution.py:272
  284.1 82.4 %all-gather.13.cloned.1.call-start = ((), (), s32[]{:S(2)}) async-start(), calls=%async_computation.6 | async-start | bytes 1327104 | tf_op jit(solution)/shard_map/all_gather | solution.py:425
  286.6 20.0 %collective-permute-start.21 = (bf16[400,768]{1,0:T(8,128)(2,1)S(1)}, bf16[400,768]{1,0:T(8,128)(2,1)S(1)}, u32[]{:S(2)}, u32[]{:S(2)}) collective-permute-start(bf16[400,768]{1,0:T(8,128)(2,1)S(1)} %get-tuple-element.100), channel_id=1, source_target_pairs={{0,8},{4,12},{8,0},{12,4},{16,24},{20,28},{24,16},{28,20},{1,9},{5... | collective-permute-start | bytes 1843208 | tf_op jit(solution)/shard_map/ppermute | solution.py:275
  288.1 31.2 %collective-permute-start.22 = (bf16[400,768]{1,0:T(8,128)(2,1)S(1)}, bf16[400,768]{1,0:T(8,128)(2,1)S(1)}, u32[]{:S(2)}, u32[]{:S(2)}) collective-permute-start(bf16[400,768]{1,0:T(8,128)(2,1)S(1)} %get-tuple-element.102), channel_id=1, source_target_pairs={{0,16},{4,20},{8,24},{12,28},{16,0},{20,4},{24,8},{28,12},{1,17},{... | collective-permute-start | bytes 1843208 | tf_op jit(solution)/shard_map/ppermute | solution.py:275
  289.6 29.8 %collective-permute-start.23 = (bf16[400,768]{1,0:T(8,128)(2,1)S(1)}, bf16[400,768]{1,0:T(8,128)(2,1)S(1)}, u32[]{:S(2)}, u32[]{:S(2)}) collective-permute-start(bf16[400,768]{1,0:T(8,128)(2,1)S(1)} %get-tuple-element.101), channel_id=1, source_target_pairs={{0,24},{4,28},{8,16},{12,20},{16,8},{20,12},{24,0},{28,4},{1,25},{... | collective-permute-start | bytes 1843208 | tf_op jit(solution)/shard_map/ppermute | solution.py:275
  321.1 21.3 %copy-start.42 = (s32[512]{0:T(512)S(1)}, s32[512]{0:T(512)}, u32[]{:S(2)}) copy-start(s32[512]{0:T(512)} %copy-done.41) | copy-start | bytes 6148
  321.1 21.3 %copy-start.44 = (s32[4,256]{1,0:T(4,128)S(1)}, s32[4,256]{1,0:T(4,128)}, u32[]{:S(2)}) copy-start(s32[4,256]{1,0:T(4,128)} %param.15) | copy-start | bytes 12292
  321.2 14.5 %collective-permute-start.24 = (bf16[112,768]{1,0:T(8,128)(2,1)S(1)}, bf16[112,768]{1,0:T(8,128)(2,1)S(1)}, u32[]{:S(2)}, u32[]{:S(2)}) collective-permute-start(bf16[112,768]{1,0:T(8,128)(2,1)S(1)} %get-tuple-element.117), channel_id=1, source_target_pairs={{0,1},{1,0},{2,3},{3,2},{4,5},{5,4},{6,7},{7,6},{8,9},{9,8},{10,11... | collective-permute-start | bytes 516104 | tf_op jit(solution)/shard_map/ppermute | solution.py:278
  328.7 12.8 %collective-permute-start.25 = (bf16[112,768]{1,0:T(8,128)(2,1)S(1)}, bf16[112,768]{1,0:T(8,128)(2,1)S(1)}, u32[]{:S(2)}, u32[]{:S(2)}) collective-permute-start(bf16[112,768]{1,0:T(8,128)(2,1)S(1)} %get-tuple-element.118), channel_id=1, source_target_pairs={{0,2},{1,3},{2,0},{3,1},{4,6},{5,7},{6,4},{7,5},{8,10},{9,11},{10,... | collective-permute-start | bytes 516104 | tf_op jit(solution)/shard_map/ppermute | solution.py:278
  328.7 12.8 %collective-permute-start.26 = (bf16[112,768]{1,0:T(8,128)(2,1)S(1)}, bf16[112,768]{1,0:T(8,128)(2,1)S(1)}, u32[]{:S(2)}, u32[]{:S(2)}) collective-permute-start(bf16[112,768]{1,0:T(8,128)(2,1)S(1)} %concatenate.18), channel_id=1, source_target_pairs={{0,3},{1,2},{2,1},{3,0},{4,7},{5,6},{6,5},{7,4},{8,11},{9,10},{10,... | collective-permute-start | bytes 516104 | tf_op jit(solution)/shard_map/ppermute | solution.py:278
  368.3 2.0 copy-start.1
  (20 other events, 17.9 us)
Sparse Core Ops, SparseCore 0:
  11.7 49.4 reduce-scatter.2
  64.0 47.3 reduce-scatter.4
  178.4 47.4 all-gather.10
  227.9 46.8 all-gather.8
  284.2 46.7 all-gather.14
  342.5 23.9 all-gather.12
